TPU v7x, 32 devices: a whole 2x2x4 slice. The times are simulated.
32 devices in a mesh: blk: 4 (over z), rep: 8 (over y, x, core).
Axes of the slice: x: 2, y: 2, z: 4, core: 2. Of those that a mesh axis runs over, the one named last changes fastest.
Arguments:
- photo_features: bfloat16 [8, 2048, 1152], P('rep', 'blk'), may hold values from -6 to 6
- wording_features: bfloat16 [8, 2048, 1152], P('rep', 'blk'), may hold values from -6 to 6
- partner_wording_slot: int32 [8, 2048], P('rep', 'blk'), may hold values from 0 to 2047, each once within a row
- photo_projector_weights: bfloat16 [1152, 1152], replicated, may hold values from -0.1875 to 0.1875
- wording_projector_weights: bfloat16 [1152, 1152], replicated, may hold values from -0.1875 to 0.1875
- learned_inverse_heat: float32 [1], replicated, may hold values from 4 to 12
- offset_term: float32 [1], replicated, may hold values from -3 to -1
Outputs:
- grad_img_head: float32 [1152, 1152], replicated
- grad_txt_head: float32 [1152, 1152], replicated
Inputs may be any that keep to these rules, and one draw needn't show every extreme that they name: `partner_wording_slot`: within each group the 2048 images name distinct texts of that group.
All inputs are finite; a program needn't handle non-finite values.
Results may differ from a plain program's by a relative error of at most 0.0029.
Values may be sent and summed in bfloat16 or wider, within the bound.
A program may use at most 128 MiB of HBM per device.

v0:
```python
import jax
import jax.numpy as jnp
from jax import lax
from jax.sharding import PartitionSpec as P

STEPS = 4


epsilon = 1e-06
criterion_prefactor = 0.0625


def from_behind(array, axis, by):
    count = lax.axis_size(axis)
    return lax.ppermute(array, axis, [(i, (i + by) % count) for i in range(count)])


def normalize(features, head):
    projected = jnp.dot(features, head, preferred_element_type=jnp.float32)
    inverse = lax.rsqrt(jnp.sum(projected * projected, axis=-1, keepdims=True) + epsilon)
    unit = projected * inverse
    return (unit, unit.astype(jnp.bfloat16), inverse)


def unnormalize(unit, inverse, upstream):
    inner = jnp.sum(unit * upstream, axis=-1, keepdims=True)
    return (inverse * (upstream - unit * inner)).astype(jnp.bfloat16)


def across_rows(left, right):
    return lax.dot_general(
        left, right, (((0,), (0,)), ((), ())), preferred_element_type=jnp.float32
    )


def local(
    photo_features,
    wording_features,
    partner_wording_slot,
    photo_projector_weights,
    wording_projector_weights,
    learned_inverse_heat,
    offset_term,
):
    image_rows = photo_features[0]
    text_rows = wording_features[0]
    targets = partner_wording_slot[0]
    row_count = image_rows.shape[0]
    block_count = lax.axis_size("blk")
    position = lax.axis_index("blk")
    img_unit, img_low, img_inv = normalize(image_rows, photo_projector_weights)
    txt_unit, txt_low, txt_inv = normalize(text_rows, wording_projector_weights)
    exponentiated_heat = learned_inverse_heat[0] * criterion_prefactor
    offsets = jnp.arange(row_count, dtype=jnp.int32)
    d_img = jnp.zeros((row_count, txt_low.shape[1]), jnp.float32)
    panel = txt_low
    partial_value = jnp.zeros((row_count, txt_low.shape[1]), jnp.float32)
    for step_index in range(STEPS):
        if step_index > 0:
            panel = from_behind(panel, "blk", 1)
            partial_value = from_behind(partial_value, "blk", 1)
        cosine_agreement_table = lax.dot_general(
            img_low, panel, (((1,), (1,)), ((), ())), preferred_element_type=jnp.float32
        )
        unbounded_pairwise_array = learned_inverse_heat[0] * cosine_agreement_table + offset_term[0]
        columns = (position - step_index) % block_count * row_count + offsets
        diagonal_label = (targets[:, None] == columns[None, :]).astype(jnp.float32)
        submatrix_block_piece = (
            exponentiated_heat * (jax.nn.sigmoid(unbounded_pairwise_array) - diagonal_label)
        ).astype(jnp.bfloat16)
        d_img = d_img + jnp.dot(submatrix_block_piece, panel, preferred_element_type=jnp.float32)
        partial_value = partial_value + across_rows(submatrix_block_piece, img_low)
    d_txt = from_behind(partial_value, "blk", -(STEPS - 1))
    grad_img = across_rows(image_rows, unnormalize(img_unit, img_inv, d_img))
    grad_txt = across_rows(text_rows, unnormalize(txt_unit, txt_inv, d_txt))
    grad_img, grad_txt = lax.psum((grad_img, grad_txt), ("blk", "rep"))
    return (grad_img, grad_txt)


def solution(mesh):
    placed = (P("rep", "blk", None), P("rep", "blk", None), P("rep", "blk"), P(), P(), P(), P())
    return jax.shard_map(local, mesh=mesh, in_specs=placed, out_specs=(P(), P()), check_vma=False)
```

profile of v0, /device:TPU:1, one launch (start us, length us, event | category | flops | bytes accessed | tf_op | source)
XLA Modules:
  0.0 569.7 jit_solution(16146102414945248000)
XLA Ops:
  7.2 1.7 copy-done
  8.9 3.4 multiply_reduce_fusion.3
  12.3 2.0 multiply_reduce_fusion.2
  15.8 1.2 multiply_convert_fusion.2
  17.1 2.4 fusion.31
  19.4 2.3 fusion.43
  21.7 2.1 collective-permute-start.3
  23.9 1.3 collective-permute-start
  25.2 77.3 %collective-permute-done = bf16[512,1152]{1,0:T(8,128)(2,1)} collective-permute-done((bf16[512,1152]{1,0:T(8,128)(2,1)}, bf16[512,1152]{1,0:T(8,128)(2,1)}, u32[]{:S(2)}, u32[]{:S(2)}) %collective-permute-start) | collective-permute-done | bytes 1179680 | tf_op jit(solution)/shard_map/ppermute | solution.py:15
  102.5 2.4 fusion.30
  104.8 4.1 convolution_add_fusion
  109.0 0.4 collective-permute-start.1
  109.4 78.5 %collective-permute-done.1 = bf16[512,1152]{1,0:T(8,128)(2,1)} collective-permute-done((bf16[512,1152]{1,0:T(8,128)(2,1)}, bf16[512,1152]{1,0:T(8,128)(2,1)}, u32[]{:S(2)}, u32[]{:S(2)}) %collective-permute-start.1) | collective-permute-done | bytes 1179680 | tf_op jit(solution)/shard_map/ppermute | solution.py:15
  187.9 2.4 fusion.29
  190.3 0.9 fusion.44
  191.2 3.4 add.151
  194.6 78.0 %collective-permute-done.2 = bf16[512,1152]{1,0:T(8,128)(2,1)} collective-permute-done((bf16[512,1152]{1,0:T(8,128)(2,1)}, bf16[512,1152]{1,0:T(8,128)(2,1)}, u32[]{:S(2)}, u32[]{:S(2)}) %collective-permute-start.2) | collective-permute-done | bytes 1179680 | tf_op jit(solution)/shard_map/ppermute | solution.py:15
  272.6 2.4 fusion.28
  274.9 0.9 fusion.45
  275.9 2.1 add.152
  277.9 0.2 collective-permute-start.6
  278.2 2.1 fusion.42
  280.3 2.2 convolution_add_fusion.3
  282.5 2.3 convolution_add_fusion.2
  284.9 2.4 multiply_reduce_fusion.1
  287.3 4.5 convolution_bitcast_fusion.1
  291.7 37.9 %collective-permute-done.6 = f32[512,1152]{1,0:T(8,128)S(1)} collective-permute-done((f32[512,1152]{1,0:T(8,128)S(1)}, f32[512,1152]{1,0:T(8,128)S(1)}, u32[]{:S(2)}, u32[]{:S(2)}) %collective-permute-start.6) | collective-permute-done | bytes 2359328 | tf_op jit(solution)/shard_map/ppermute | solution.py:15
  329.6 0.5 multiply_reduce_fusion
  330.1 4.4 convolution_bitcast_fusion
  334.5 214.5 %all-reduce.3.cloned.1.call-done = (f32[1152,1152]{0,1:T(8,128)}, f32[1152,1152]{0,1:T(8,128)}) async-done(((f32[1152,1152]{0,1:T(8,128)}, f32[1152,1152]{0,1:T(8,128)}), (f32[1152,1152]{0,1:T(8,128)}, f32[1152,1152]{0,1:T(8,128)})) %all-reduce.3.cloned.1.call-update) | async-done | bytes 10616848 | tf_op jit(solution)/shard_map/psum | solution.py:76
  549.0 6.9 %copy.10 = f32[1152,1152]{1,0:T(8,128)} copy(f32[1152,1152]{0,1:T(8,128)} %get-tuple-element.5) | data formatting | bytes 10616832
  555.8 7.0 %copy.9 = f32[1152,1152]{1,0:T(8,128)} copy(f32[1152,1152]{0,1:T(8,128)} %get-tuple-element.4) | data formatting | bytes 10616832
  (44 shorter events, 0.4 us)
Async XLA Ops:
  7.2 1.8 copy-start
  7.2 541.8 %all-reduce.3.cloned.1.call-start = ((), (), s32[]{:S(2)}) async-start(), calls=%async_computation | async-start | bytes 21233664 | tf_op jit(solution)/shard_map/psum | solution.py:76
  8.9 3.4 copy-start.11
  8.9 3.4 copy-start.13
  12.3 3.3 copy-start.2
  15.8 1.2 copy-start.14
  19.4 2.3 copy-start.4
  21.7 83.1 %collective-permute-start.3 = (f32[512,1152]{1,0:T(8,128)}, f32[512,1152]{1,0:T(8,128)}, u32[]{:S(2)}, u32[]{:S(2)}) collective-permute-start(f32[512,1152]{1,0:T(8,128)} %fusion.43), channel_id=1, source_target_pairs={{0,8},{8,16},{16,24},{24,0},{1,9},{9,17},{17,25},{25,1},{2,10},{10... | collective-permute-start | bytes 7077896 | tf_op jit(solution)/shard_map/ppermute | solution.py:15
  23.9 78.6 %collective-permute-start = (bf16[512,1152]{1,0:T(8,128)(2,1)}, bf16[512,1152]{1,0:T(8,128)(2,1)}, u32[]{:S(2)}, u32[]{:S(2)}) collective-permute-start(bf16[512,1152]{1,0:T(8,128)(2,1)} %multiply_convert_fusion.2), channel_id=1, source_target_pairs={{0,8},{8,16},{16,24},{24,0},{1,9},{9,17},{17,25},{25,1},{2,10},{10... | collective-permute-start | bytes 3538952 | tf_op jit(solution)/shard_map/ppermute | solution.py:15
  104.8 4.2 copy-start.8
  109.0 82.2 %collective-permute-start.4 = (f32[512,1152]{1,0:T(8,128)}, f32[512,1152]{1,0:T(8,128)}, u32[]{:S(2)}, u32[]{:S(2)}) collective-permute-start(f32[512,1152]{1,0:T(8,128)} %convolution_add_fusion), channel_id=1, source_target_pairs={{0,8},{8,16},{16,24},{24,0},{1,9},{9,17},{17,25},{25,1},{2,10},{10... | collective-permute-start | bytes 7077896 | tf_op jit(solution)/shard_map/ppermute | solution.py:15
  109.0 78.9 %collective-permute-start.1 = (bf16[512,1152]{1,0:T(8,128)(2,1)}, bf16[512,1152]{1,0:T(8,128)(2,1)}, u32[]{:S(2)}, u32[]{:S(2)}) collective-permute-start(bf16[512,1152]{1,0:T(8,128)(2,1)} %collective-permute-done), channel_id=1, source_target_pairs={{0,8},{8,16},{16,24},{24,0},{1,9},{9,17},{17,25},{25,1},{2,10},{10... | collective-permute-start | bytes 3538952 | tf_op jit(solution)/shard_map/ppermute | solution.py:15
  190.3 0.9 copy-start.6
  194.6 81.2 %collective-permute-start.5 = (f32[512,1152]{1,0:T(8,128)}, f32[512,1152]{1,0:T(8,128)}, u32[]{:S(2)}, u32[]{:S(2)}) collective-permute-start(f32[512,1152]{1,0:T(8,128)} %add.151), channel_id=1, source_target_pairs={{0,8},{8,16},{16,24},{24,0},{1,9},{9,17},{17,25},{25,1},{2,10},{10... | collective-permute-start | bytes 7077896 | tf_op jit(solution)/shard_map/ppermute | solution.py:15
  194.6 78.0 %collective-permute-start.2 = (bf16[512,1152]{1,0:T(8,128)(2,1)}, bf16[512,1152]{1,0:T(8,128)(2,1)}, u32[]{:S(2)}, u32[]{:S(2)}) collective-permute-start(bf16[512,1152]{1,0:T(8,128)(2,1)} %collective-permute-done.1), channel_id=1, source_target_pairs={{0,8},{8,16},{16,24},{24,0},{1,9},{9,17},{17,25},{25,1},{2,10},{10... | collective-permute-start | bytes 3538952 | tf_op jit(solution)/shard_map/ppermute | solution.py:15
  275.8 2.3 copy-start.5
  277.9 2.4 copy-start.9
  277.9 51.7 %collective-permute-start.6 = (f32[512,1152]{1,0:T(8,128)S(1)}, f32[512,1152]{1,0:T(8,128)S(1)}, u32[]{:S(2)}, u32[]{:S(2)}) collective-permute-start(f32[512,1152]{1,0:T(8,128)S(1)} %add.152), channel_id=1, source_target_pairs={{0,8},{8,16},{16,24},{24,0},{1,9},{9,17},{17,25},{25,1},{2,10},{10... | collective-permute-start | bytes 7077896 | tf_op jit(solution)/shard_map/ppermute | solution.py:15
  280.3 2.2 copy-start.7
  282.5 2.3 copy-start.3
  284.9 2.4 copy-start.10
  291.7 38.3 %copy-start.12 = (bf16[1,512,1152]{2,1,0:T(8,128)(2,1)S(1)}, bf16[1,512,1152]{2,1,0:T(8,128)(2,1)}, u32[]{:S(2)}) copy-start(bf16[1,512,1152]{2,1,0:T(8,128)(2,1)} %param.8) | copy-start | bytes 3538948
  555.8 7.0 %copy-start.1 = (bf16[1152,1152]{1,0:T(8,128)(2,1)S(1)}, bf16[1152,1152]{1,0:T(8,128)(2,1)}, u32[]{:S(2)}) copy-start(bf16[1152,1152]{1,0:T(8,128)(2,1)} %param.10) | copy-start | bytes 7962628
Sparse Core Ops, SparseCore 0:
  334.6 214.3 all-reduce.2
where the time goes:
time: 572 us; the launch traced here: 570 us
  waiting for transfers between devices  486 us (85%)
  matrix products  40.8 us (7%)
  local copies, waits for them, and re-layouts  15.6 us (3%)
  between operations  15.6 us (3%)
  other arithmetic  7.37 us (1%)
    ppermute x7, waiting for transfers between devices, from_behind(): lax.ppermute(array, axis, [(i, (i + by) % count) for i in range(count)])  272 us
    psum x1, waiting for transfers between devices, local(): grad_img, grad_txt = lax.psum((grad_img, grad_txt), ('blk', 'rep'))  214 us
    dot_general x6, matrix products, across_rows(): lax.dot_general(left, right, (((0,), (0,)), ((), ())), preferred_element_...  17.1 us
    unnamed x32, local copies, waits for them, and re-layouts  15.6 us
  transfers between devices with their start and end apart: 8, of which 5 were waited for; matrix products, arithmetic and copies ran while one was open for 4% of the time, Pallas kernels for 0%

commit v1 on v0

--- a/solution.py
+++ b/solution.py
@@ -1,9 +1,16 @@
+import functools
+
 import jax
 import jax.numpy as jnp
 from jax import lax
+from jax.experimental import pallas as pl
+from jax.experimental.pallas import tpu as pltpu
 from jax.sharding import PartitionSpec as P
 
 STEPS = 4
+MESH = pl.DeviceIdType.MESH
+CHUNKS = 3
+PAD = 16
 
 
 epsilon = 1e-06
@@ -33,7 +40,7 @@
     )
 
 
-def local(
+def ring_local(
     photo_features,
     wording_features,
     partner_wording_slot,
@@ -77,6 +84,244 @@
     return (grad_img, grad_txt)
 
 
+def reduce_kernel(
+    n_z, img_ref, txt_ref, out_ref, got0, acc, s1, r1, s2, r2, r3, send, recv
+):
+    rows, cols = img_ref.shape
+    width = cols // CHUNKS
+    half, quarter = rows // 2, rows // 4
+    piece = quarter // n_z
+    padded = out_ref.shape[4]
+    z, r = lax.axis_index("blk"), lax.axis_index("rep")
+    core, x, y = r % 2, (r // 2) % 2, r // 4
+    a1 = x + core * (y - x)
+    a2 = y + core * (x - y)
+    sibling = r + 1 - 2 * core
+    p1 = r + (2 + 2 * core) * (1 - 2 * a1)
+    p2 = r + (4 - 2 * core) * (1 - 2 * a2)
+    turn = [lax.rem(z + d, n_z) for d in range(n_z)]
+    back = [lax.rem(z - d + n_z, n_z) for d in range(n_z)]
+
+    barrier = pltpu.get_barrier_semaphore()
+    for who in [(z, sibling), (z, p1), (z, p2)] + [(turn[d], r) for d in range(1, n_z)]:
+        pl.semaphore_signal(barrier, inc=1, device_id=who, device_id_type=MESH)
+    pl.semaphore_wait(barrier, 2 + n_z)
+
+    def span(c):
+        return pl.ds(c * width, width)
+
+    def copy(src, dst, c, slot, who):
+        return pltpu.make_async_remote_copy(
+            src_ref=src,
+            dst_ref=dst,
+            send_sem=send.at[c, slot],
+            recv_sem=recv.at[c, slot],
+            device_id=who,
+            device_id_type=MESH,
+        )
+
+    def of(start, size, step):
+        return pl.ds(pl.multiple_of(start, step), size)
+
+    keep1 = of(a1 * half, half, 16)
+    give1 = of((1 - a1) * half, half, 16)
+    base2 = a1 * half + a2 * quarter
+    keep2 = of(base2, quarter, 8)
+    give2 = of(a1 * half + (1 - a2) * quarter, quarter, 8)
+    mine2 = of(a2 * quarter, quarter, 8)
+
+    def c0(c, ref):
+        return copy(ref.at[:, span(c)], got0.at[:, span(c)], c, 0, (z, sibling))
+
+    def c1(c):
+        return copy(s1.at[:, span(c)], r1.at[:, span(c)], c, 1, (z, p1))
+
+    def c2(c):
+        return copy(s2.at[:, span(c)], r2.at[:, span(c)], c, 2, (z, p2))
+
+    def c3(c, d):
+        src = acc.at[of(base2 + turn[d] * piece, piece, 8), span(c)]
+        return copy(src, r3.at[d, :, span(c)], c, 2 + d, (turn[d], r))
+
+    def g3(c, d):
+        slot = out_ref.at[core, a1, a2, z, :, span(c)]
+        return copy(slot, slot, c, 1 + n_z + d, (turn[d], r))
+
+    def g3_in(c, d):
+        slot = out_ref.at[core, a1, a2, back[d], :, span(c)]
+        return copy(slot, slot, c, 1 + n_z + d, (turn[d], r))
+
+    def g2(c, part):
+        slot = out_ref.at[core, a1, part, :, :, span(c)]
+        return copy(slot, slot, c, 1 + 2 * n_z, (z, p2))
+
+    def g1(c, part):
+        slot = out_ref.at[core, part, :, :, :, span(c)]
+        return copy(slot, slot, c, 2 + 2 * n_z, (z, p1))
+
+    def g0(c, part):
+        slot = out_ref.at[part, :, :, :, :, span(c)]
+        return copy(slot, slot, c, 3 + 2 * n_z, (z, sibling))
+
+    def stage0(c):
+        @pl.when(core == 0)
+        def _():
+            c0(c, txt_ref).start()
+
+        @pl.when(core == 1)
+        def _():
+            c0(c, img_ref).start()
+
+    def stage1(c):
+        c0(c, img_ref).wait()
+
+        def add(ref):
+            s1[:, span(c)] = (ref[give1, span(c)] + got0[give1, span(c)]).astype(s1.dtype)
+            c1(c).start()
+            acc[keep1, span(c)] = ref[keep1, span(c)] + got0[keep1, span(c)]
+
+        @pl.when(core == 0)
+        def _():
+            add(img_ref)
+
+        @pl.when(core == 1)
+        def _():
+            add(txt_ref)
+
+    def stage2(c):
+        c1(c).wait()
+        other2 = of((1 - a2) * quarter, quarter, 16)
+        s2[:, span(c)] = (acc[give2, span(c)] + r1[other2, span(c)].astype(jnp.float32)).astype(s2.dtype)
+        c2(c).start()
+        own2 = of(a2 * quarter, quarter, 16)
+        acc[keep2, span(c)] = acc[keep2, span(c)] + r1[own2, span(c)].astype(jnp.float32)
+
+    def stage3(c):
+        c2(c).wait()
+        acc[keep2, span(c)] = acc[keep2, span(c)] + r2[:, span(c)].astype(jnp.float32)
+        for d in range(1, n_z):
+            c3(c, d).start()
+
+    def stage4(c):
+        total = acc[of(base2 + z * piece, piece, 8), span(c)]
+        for d in range(1, n_z):
+            c3(c, d).wait()
+            total = total + r3[d, :, span(c)]
+        if padded > piece:
+            total = jnp.concatenate([total, jnp.zeros((padded - piece, width), jnp.float32)], axis=0)
+        out_ref[core, a1, a2, z, :, span(c)] = total.astype(out_ref.dtype)
+        for d in range(1, n_z):
+            g3(c, d).start()
+
+    def stage5(c):
+        for d in range(1, n_z):
+            g3_in(c, d).wait_recv()
+        g2(c, a2).start()
+
+    def stage6(c):
+        g2(c, 1 - a2).wait_recv()
+        g1(c, a1).start()
+
+    def stage7(c):
+        g1(c, 1 - a1).wait_recv()
+        g0(c, core).start()
+
+    def stage8(c):
+        g0(c, 1 - core).wait_recv()
+        for d in range(1, n_z):
+            g3(c, d).wait_send()
+        g2(c, a2).wait_send()
+        g1(c, a1).wait_send()
+        g0(c, core).wait_send()
+
+    for c in range(CHUNKS):
+        stage0(c)
+    stages = [stage1, stage2, stage3, stage4, stage5, stage6, stage7, stage8]
+    for tick in range(CHUNKS + len(stages) - 1):
+        for at in range(len(stages)):
+            if 0 <= tick - at < CHUNKS:
+                stages[at](tick - at)
+
+
+def reduce_all(grad_img, grad_txt, n_z):
+    rows, cols = grad_img.shape
+    half, quarter = rows // 2, rows // 4
+    piece = quarter // n_z
+    padded = -(-piece // PAD) * PAD
+    low = jnp.bfloat16
+    out = pl.pallas_call(
+        functools.partial(reduce_kernel, n_z),
+        out_shape=jax.ShapeDtypeStruct((2, 2, 2, n_z, padded, cols), low),
+        in_specs=[pl.BlockSpec(memory_space=pltpu.VMEM)] * 2,
+        out_specs=pl.BlockSpec(memory_space=pltpu.VMEM),
+        scratch_shapes=[
+            pltpu.VMEM((rows, cols), jnp.float32),
+            pltpu.VMEM((rows, cols), jnp.float32),
+            pltpu.VMEM((half, cols), low),
+            pltpu.VMEM((half, cols), low),
+            pltpu.VMEM((quarter, cols), low),
+            pltpu.VMEM((quarter, cols), low),
+            pltpu.VMEM((n_z, piece, cols), jnp.float32),
+            pltpu.SemaphoreType.DMA((CHUNKS, 4 + 2 * n_z)),
+            pltpu.SemaphoreType.DMA((CHUNKS, 4 + 2 * n_z)),
+        ],
+        compiler_params=pltpu.CompilerParams(
+            collective_id=0, has_side_effects=True, vmem_limit_bytes=50 * 1024 * 1024
+        ),
+        cost_estimate=pl.CostEstimate(flops=10**9, bytes_accessed=10**8, transcendentals=0),
+    )(grad_img, grad_txt)
+    by_core = [out[c, :, :, :, :piece].astype(jnp.float32) for c in range(2)]
+    return tuple(part.reshape(rows, cols) for part in by_core)
+
+
+def tile_local(
+    photo_features,
+    wording_features,
+    partner_wording_slot,
+    photo_projector_weights,
+    wording_projector_weights,
+    learned_inverse_heat,
+    offset_term,
+):
+    position = lax.axis_index("blk")
+    row_count = photo_features.shape[1]
+    swap1 = [(i, i ^ 1) for i in range(4)]
+    swap2 = [(i, i ^ 2) for i in range(4)]
+    photos = [photo_features[0], lax.ppermute(photo_features[0], "blk", swap1)]
+    wordings = [wording_features[0], lax.ppermute(wording_features[0], "blk", swap2)]
+    targets = [partner_wording_slot[0], lax.ppermute(partner_wording_slot[0], "blk", swap1)]
+    text_block = [position, (position + 2) % 4]
+    heat, offset = learned_inverse_heat[0], offset_term[0]
+    offsets = jnp.arange(row_count, dtype=jnp.int32)
+    images = [normalize(rows, photo_projector_weights) for rows in photos]
+    texts = [normalize(rows, wording_projector_weights) for rows in wordings]
+
+    def resid(a, b):
+        cosine = lax.dot_general(
+            images[a][1], texts[b][1], (((1,), (1,)), ((), ())), preferred_element_type=jnp.float32
+        )
+        label = (targets[a][:, None] == (text_block[b] * row_count + offsets)[None, :]).astype(jnp.float32)
+        return (heat * criterion_prefactor * (jax.nn.sigmoid(heat * cosine + offset) - label)).astype(jnp.bfloat16)
+
+    pieces = [[resid(a, b) for b in range(2)] for a in range(2)]
+
+    def grad_of(rows, own, upstream):
+        return sum(
+            across_rows(rows[k], unnormalize(own[k][0], own[k][2], upstream[k])) for k in range(2)
+        )
+
+    d_img = [
+        sum(jnp.dot(pieces[a][b], texts[b][1], preferred_element_type=jnp.float32) for b in range(2))
+        for a in range(2)
+    ]
+    d_txt = [sum(across_rows(pieces[a][b], images[a][1]) for a in range(2)) for b in range(2)]
+    grad_img = grad_of(photos, images, d_img)
+    grad_txt = grad_of(wordings, texts, d_txt)
+    return reduce_all(grad_img, grad_txt, 4)
+
+
 def solution(mesh):
     placed = (P("rep", "blk", None), P("rep", "blk", None), P("rep", "blk"), P(), P(), P(), P())
-    return jax.shard_map(local, mesh=mesh, in_specs=placed, out_specs=(P(), P()), check_vma=False)
+    tiled = mesh.shape["blk"] == STEPS == 4 and mesh.shape["rep"] == 8
+    body = tile_local if tiled else ring_local
+    return jax.shard_map(body, mesh=mesh, in_specs=placed, out_specs=(P(), P()), check_vma=False)

time: 572 us -> 194 us (0.34)
  waiting for transfers between devices: 486 us -> 38.4 us
  Pallas kernels: 0 us -> 93 us
  between operations: 15.6 us -> 2.16 us
  local copies, waits for them, and re-layouts: 15.6 us -> 4.19 us
    ppermute x7 -> x3, waiting for transfers between devices: 272 us -> 38.4 us  [the longest x1 38.4 us: tile_local(): photos = [photo_features[0], lax.ppermute(photo_features[0], 'blk', swap1)]]
    psum x1 -> x0, waiting for transfers between devices: 214 us -> none  [local(): grad_img, grad_txt = lax.psum((grad_img, grad_txt), ('blk', 'rep'))]
    pallas_call x0 -> x1, Pallas kernels: none -> 93 us  [reduce_all(): pl.pallas_call(functools.partial(reduce_kernel, n_z), out_shape=jax.Shape...]
    unnamed x32 -> x14, local copies, waits for them, and re-layouts: 15.6 us -> 1.22 us
    dot_general x8, matrix products: 18.4 us -> 8.31 us  [the longest x4 4.55 us: resid(): lax.dot_general(images[a][1], texts[b][1], (((1,), (1,)), ((), ())), pref...]
    dot_general x2 -> x4, matrix products: 5.32 us -> 15.1 us  [normalize(): projected = jnp.dot(features, head, preferred_element_type=jnp.float32)]
    convert_element_type x0 -> x2, other arithmetic: none -> 5.85 us  [reduce_all(): by_core = [out[c, :, :, :, :piece].astype(jnp.float32) for c in range(2)]]
    dot_general x6 -> x8, matrix products: 17.1 us -> 19.6 us  [across_rows(): lax.dot_general(left, right, (((0,), (0,)), ((), ())), preferred_element_...]
  transfers between devices with their start and end apart: 8 -> 3, of which waited for: 5 -> 1; matrix products, arithmetic and copies ran while one was open for 4% -> 11% of each run, Pallas kernels for 0% -> 0%
where the time goes in v1:
time: 194 us; the launch traced here: 192 us
  Pallas kernels  93 us (48%)
  matrix products  43 us (22%)
  waiting for transfers between devices  38.4 us (20%)
  other arithmetic  6.63 us (3%)
  starting transfers between devices  4.67 us (2%)
  local copies, waits for them, and re-layouts  4.19 us (2%)
  between operations  2.16 us (1%)
    pallas_call x1, Pallas kernels, reduce_all(): pl.pallas_call(functools.partial(reduce_kernel, n_z), out_shape=jax.Shape...  93 us
    ppermute x1, waiting for transfers between devices, tile_local(): photos = [photo_features[0], lax.ppermute(photo_features[0], 'blk', swap1)]  38.4 us
    dot_general x8, matrix products, across_rows(): lax.dot_general(left, right, (((0,), (0,)), ((), ())), preferred_element_...  19.6 us
    dot_general x4, matrix products, normalize(): projected = jnp.dot(features, head, preferred_element_type=jnp.float32)  15.1 us
    convert_element_type x2, other arithmetic, reduce_all(): by_core = [out[c, :, :, :, :piece].astype(jnp.float32) for c in range(2)]  5.85 us
    dot_general x4, matrix products, resid(): lax.dot_general(images[a][1], texts[b][1], (((1,), (1,)), ((), ())), pref...  4.55 us
  transfers between devices with their start and end apart: 3, of which 1 were waited for; matrix products, arithmetic and copies ran while one was open for 11% of the time, Pallas kernels for 0%

profile of v1, /device:TPU:1, one launch (start us, length us, event | category | flops | bytes accessed | tf_op | source)
XLA Modules:
  0.0 192.1 jit_solution(8987034074002564974)
XLA Ops:
  0.6 2.2 %collective-permute-start.1 = (bf16[512,1152]{1,0:T(8,128)(2,1)}, bf16[512,1152]{1,0:T(8,128)(2,1)}, u32[]{:S(2)}, u32[]{:S(2)}) collective-permute-start(bf16[512,1152]{1,0:T(8,128)(2,1)} %bitcast.68), channel_id=1, source_target_pairs={{0,8},{8,0},{16,24},{24,16},{1,9},{9,1},{17,25},{25,17},{2,10},{10... | collective-permute-start | bytes 3538952 | tf_op jit(solution)/shard_map/ppermute | solution.py:290
  2.8 2.3 %collective-permute-start = (bf16[512,1152]{1,0:T(8,128)(2,1)}, bf16[512,1152]{1,0:T(8,128)(2,1)}, u32[]{:S(2)}, u32[]{:S(2)}) collective-permute-start(bf16[512,1152]{1,0:T(8,128)(2,1)} %bitcast.69), channel_id=1, source_target_pairs={{0,16},{8,24},{16,0},{24,8},{1,17},{9,25},{17,1},{25,9},{2,18},{10... | collective-permute-start | bytes 3538952 | tf_op jit(solution)/shard_map/ppermute | solution.py:291
  5.3 4.5 %multiply_reduce_fusion.7 = (f32[512]{0:T(512)S(1)}, f32[512,1152]{1,0:T(8,128)}) fusion(bf16[1152,1152]{1,0:T(8,128)(2,1)S(1)} %copy-done, bf16[1,512,1152]{2,1,0:T(8,128)(2,1)} %param.7), kind=kOutput, calls=%fused_computation.21 | convolution fusion | flops 1360133632 | bytes 6195200 | tf_op jit(solution)/shard_map/dot_general | solution.py:26
  11.2 4.2 %multiply_reduce_fusion.6 = (f32[512]{0:T(512)S(1)}, f32[512,1152]{1,0:T(8,128)S(1)}) fusion(bf16[1152,1152]{1,0:T(8,128)(2,1)} %param.11, bf16[1,512,1152]{2,1,0:T(8,128)(2,1)} %param.8), kind=kOutput, calls=%fused_computation.20 | convolution fusion | flops 1360133632 | bytes 6195200 | tf_op jit(solution)/shard_map/dot_general | solution.py:26
  15.4 0.2 multiply_convert_fusion.7
  15.6 38.4 %collective-permute-done.1 = bf16[512,1152]{1,0:T(8,128)(2,1)} collective-permute-done((bf16[512,1152]{1,0:T(8,128)(2,1)}, bf16[512,1152]{1,0:T(8,128)(2,1)}, u32[]{:S(2)}, u32[]{:S(2)}) %collective-permute-start.1) | collective-permute-done | bytes 1179680 | tf_op jit(solution)/shard_map/ppermute | solution.py:290
  54.0 3.2 %multiply_reduce_fusion.3 = (f32[512]{0:T(512)S(1)}, f32[512,1152]{1,0:T(8,128)S(1)}) fusion(bf16[512,1152]{1,0:T(8,128)(2,1)} %collective-permute-done.1, bf16[1152,1152]{1,0:T(8,128)(2,1)S(1)} %copy-done), kind=kOutput, calls=%fused_computation.16 | convolution fusion | flops 1360133632 | bytes 6195200 | tf_op jit(solution)/shard_map/dot_general | solution.py:26
  57.2 0.3 multiply_convert_fusion.4
  57.6 0.3 copy-done.6
  57.9 1.1 fusion.27
  59.0 0.8 fusion.45
  59.9 0.9 fusion.47
  60.8 0.9 copy-done.5
  61.6 3.2 %multiply_reduce_fusion.5 = (f32[512]{0:T(512)S(1)}, f32[512,1152]{1,0:T(8,128)S(1)}) fusion(bf16[512,1152]{1,0:T(8,128)(2,1)} %collective-permute-done, bf16[1152,1152]{1,0:T(8,128)(2,1)S(1)} %copy-done.5), kind=kOutput, calls=%fused_computation.19 | convolution fusion | flops 1360133632 | bytes 6195200 | tf_op jit(solution)/shard_map/dot_general | solution.py:26
  64.8 0.2 multiply_convert_fusion.5
  65.0 1.1 fusion.26
  66.1 1.1 multiply_reduce_fusion.4
  67.2 0.9 fusion.48
  68.1 1.3 multiply_convert_fusion.13
  69.4 0.8 fusion.46
  70.2 1.3 multiply_reduce_fusion.1
  71.5 1.1 multiply_convert_fusion.12
  72.6 1.0 multiply_reduce_fusion.2
  73.6 1.3 multiply_reduce_fusion
  74.9 1.9 fusion.28
  76.8 2.0 %fusion.29 = f32[1152,1152]{0,1:T(8,128)S(1)} fusion(f32[512,1152]{1,0:T(8,128)S(1)} %get-tuple-element.17, f32[512,1152]{1,0:T(8,128)S(1)} %get-tuple-element.7, f32[512]{0:T(512)S(1)} %get-tuple-element.16, f32[512]{0:T(512)S(1)} %add_rsqrt_fusion.2, bf16[1,512,1152]{2,1,0:T(8,128)(2,1)S(1)} %copy-done.4), kind=kOutput, calls=%fused_computation.57 | convolution fusion | flops 1361903616 | bytes 11210752 | tf_op jit(solution)/shard_map/dot_general | solution.py:38
  78.8 5.6 %fusion.img_ref = f32[1152,1152]{1,0:T(8,128)} fusion(f32[1152,1152]{0,1:T(8,128)S(1)} %fusion.28, bf16[512,1152]{1,0:T(8,128)(2,1)} %collective-permute-done.1, f32[512,1152]{1,0:T(8,128)S(1)} %get-tuple-element.15, f32[512,1152]{1,0:T(8,128)S(1)} %get-tuple-element.13, f32[512]{0:T(512)S(1)} %get-tuple-element.14, f32[512]{0:T(512)S(1)} %add_rsqrt_fusion), kind=kOutput, calls=%fused_computation.2 | convolution fusion | flops 1363230720 | bytes 16519168 | tf_op jit(solution)/shard_map/dot_general | solution.py:38
  84.4 5.9 %fusion.1.txt_ref = f32[1152,1152]{1,0:T(8,128)} fusion(f32[1152,1152]{0,1:T(8,128)S(1)} %fusion.29, bf16[512,1152]{1,0:T(8,128)(2,1)} %collective-permute-done, f32[512,1152]{1,0:T(8,128)S(1)} %get-tuple-element.19, f32[512,1152]{1,0:T(8,128)S(1)} %get-tuple-element.9, f32[512]{0:T(512)S(1)} %get-tuple-element.18, f32[512]{0:T(512)S(1)} %add_rsqrt_fusion.1), kind=kOutput, calls=%fused_computation.3 | convolution fusion | flops 1363230720 | bytes 16519168 | tf_op jit(solution)/shard_map/dot_general | solution.py:38
  90.2 93.0 %shard_map.86 = bf16[2,2,2,4,80,1152]{5,4,3,2,1,0:T(8,128)(2,1)} custom-call(f32[1152,1152]{1,0:T(8,128)} %fusion.img_ref, f32[1152,1152]{1,0:T(8,128)} %fusion.1.txt_ref), custom_call_target="tpu_custom_call" | custom-call | flops 1000000000 | bytes 100000000 | tf_op jit(solution)/shard_map/pallas_call | solution.py:252
  183.3 3.0 %fusion.44 = (bf16[1,2,2,4,72,1152]{5,4,3,2,1,0:T(8,128)(2,1)S(1)}, bf16[1,2,2,4,72,1152]{5,4,3,2,1,0:T(8,128)(2,1)S(1)}) fusion(bf16[2,2,2,4,80,1152]{5,4,3,2,1,0:T(8,128)(2,1)} %shard_map.86), kind=kLoop, calls=%fused_computation.80 | loop fusion | bytes 10616832 | tf_op jit(solution)/shard_map/slice | solution.py:273
  186.2 2.9 %bitcast_convert_fusion.1 = f32[1152,1152]{1,0:T(8,128)} fusion(bf16[1,2,2,4,72,1152]{5,4,3,2,1,0:T(8,128)(2,1)S(1)} %get-tuple-element.3), kind=kLoop, calls=%fused_computation.9 | loop fusion | flops 1327104 | bytes 7962624 | tf_op jit(solution)/shard_map/convert_element_type | solution.py:273
  189.1 2.9 %bitcast_convert_fusion = f32[1152,1152]{1,0:T(8,128)} fusion(bf16[1,2,2,4,72,1152]{5,4,3,2,1,0:T(8,128)(2,1)S(1)} %get-tuple-element.2), kind=kLoop, calls=%fused_computation.8 | loop fusion | flops 1327104 | bytes 7962624 | tf_op jit(solution)/shard_map/convert_element_type | solution.py:273
  (21 shorter events, 0.2 us)
Async XLA Ops:
  0.6 4.7 %copy-start = (bf16[1152,1152]{1,0:T(8,128)(2,1)S(1)}, bf16[1152,1152]{1,0:T(8,128)(2,1)}, u32[]{:S(2)}) copy-start(bf16[1152,1152]{1,0:T(8,128)(2,1)} %param.10) | copy-start | bytes 7962628
  0.6 53.4 %collective-permute-start.1 = (bf16[512,1152]{1,0:T(8,128)(2,1)}, bf16[512,1152]{1,0:T(8,128)(2,1)}, u32[]{:S(2)}, u32[]{:S(2)}) collective-permute-start(bf16[512,1152]{1,0:T(8,128)(2,1)} %bitcast.68), channel_id=1, source_target_pairs={{0,8},{8,0},{16,24},{24,16},{1,9},{9,1},{17,25},{25,17},{2,10},{10... | collective-permute-start | bytes 3538952 | tf_op jit(solution)/shard_map/ppermute | solution.py:290
  2.8 57.9 %collective-permute-start = (bf16[512,1152]{1,0:T(8,128)(2,1)}, bf16[512,1152]{1,0:T(8,128)(2,1)}, u32[]{:S(2)}, u32[]{:S(2)}) collective-permute-start(bf16[512,1152]{1,0:T(8,128)(2,1)} %bitcast.69), channel_id=1, source_target_pairs={{0,16},{8,24},{16,0},{24,8},{1,17},{9,25},{17,1},{25,9},{2,18},{10... | collective-permute-start | bytes 3538952 | tf_op jit(solution)/shard_map/ppermute | solution.py:291
  5.1 63.0 %collective-permute-start.2 = (s32[512]{0:T(512)}, s32[512]{0:T(512)S(1)}, u32[]{:S(2)}, u32[]{:S(2)}) collective-permute-start(s32[512]{0:T(512)} %bitcast.70), channel_id=1, source_target_pairs={{0,8},{8,0},{16,24},{24,16},{1,9},{9,1},{17,25},{25,17},{2,10},{10... | collective-permute-start | bytes 6152 | tf_op jit(solution)/shard_map/ppermute | solution.py:292
  11.2 4.2 %copy-start.2 = (f32[512,1152]{1,0:T(8,128)S(1)}, f32[512,1152]{1,0:T(8,128)}, u32[]{:S(2)}) copy-start(f32[512,1152]{1,0:T(8,128)} %get-tuple-element.5) | copy-start | bytes 7077892
  57.2 0.7 copy-start.6
  59.9 1.8 copy-start.5
  73.6 1.3 copy-start.3
  74.9 1.9 copy-start.4
  189.1 2.9 %copy-start.1 = (bf16[1152,1152]{1,0:T(8,128)(2,1)S(1)}, bf16[1152,1152]{1,0:T(8,128)(2,1)}, u32[]{:S(2)}) copy-start(bf16[1152,1152]{1,0:T(8,128)(2,1)} %param.10) | copy-start | bytes 7962628

commit v2 on v1

--- a/solution.py
+++ b/solution.py
@@ -9,7 +9,7 @@
 
 STEPS = 4
 MESH = pl.DeviceIdType.MESH
-CHUNKS = 3
+WIDTH = 128
 PAD = 16
 
 
@@ -85,13 +85,16 @@
 
 
 def reduce_kernel(
-    n_z, img_ref, txt_ref, out_ref, got0, acc, s1, r1, s2, r2, r3, send, recv
+    n_z, xi0, xi1, xt0, xt1, di0, di1, dt0, dt1, img_ref, txt_ref,
+    give, got0, acc, s1, r1, r2, r3, pool, send, recv
 ):
     rows, cols = img_ref.shape
-    width = cols // CHUNKS
+    chunks, _, width = acc.shape
+    panels, _, wide = give.shape
+    per = chunks // panels
     half, quarter = rows // 2, rows // 4
     piece = quarter // n_z
-    padded = out_ref.shape[4]
+    padded = pool.shape[5]
     z, r = lax.axis_index("blk"), lax.axis_index("rep")
     core, x, y = r % 2, (r // 2) % 2, r // 4
     a1 = x + core * (y - x)
@@ -107,9 +110,6 @@
         pl.semaphore_signal(barrier, inc=1, device_id=who, device_id_type=MESH)
     pl.semaphore_wait(barrier, 2 + n_z)
 
-    def span(c):
-        return pl.ds(c * width, width)
-
     def copy(src, dst, c, slot, who):
         return pltpu.make_async_remote_copy(
             src_ref=src,
@@ -128,94 +128,115 @@
     base2 = a1 * half + a2 * quarter
     keep2 = of(base2, quarter, 8)
     give2 = of(a1 * half + (1 - a2) * quarter, quarter, 8)
-    mine2 = of(a2 * quarter, quarter, 8)
-
-    def c0(c, ref):
-        return copy(ref.at[:, span(c)], got0.at[:, span(c)], c, 0, (z, sibling))
+    own2 = of(a2 * quarter, quarter, 16)
+    other2 = of((1 - a2) * quarter, quarter, 16)
+
+    def c0(m):
+        return copy(give.at[m], got0.at[m], m, 0, (z, sibling))
 
     def c1(c):
-        return copy(s1.at[:, span(c)], r1.at[:, span(c)], c, 1, (z, p1))
+        return copy(s1.at[c], r1.at[c], c, 1, (z, p1))
 
     def c2(c):
-        return copy(s2.at[:, span(c)], r2.at[:, span(c)], c, 2, (z, p2))
+        return copy(acc.at[c, give2], r2.at[c], c, 2, (z, p2))
 
     def c3(c, d):
-        src = acc.at[of(base2 + turn[d] * piece, piece, 8), span(c)]
-        return copy(src, r3.at[d, :, span(c)], c, 2 + d, (turn[d], r))
-
-    def g3(c, d):
-        slot = out_ref.at[core, a1, a2, z, :, span(c)]
+        src = acc.at[c, of(base2 + turn[d] * piece, piece, 8)]
+        return copy(src, r3.at[c, d], c, 2 + d, (turn[d], r))
+
+    def g3(c, d, at):
+        slot = pool.at[c, core, a1, a2, at]
         return copy(slot, slot, c, 1 + n_z + d, (turn[d], r))
 
-    def g3_in(c, d):
-        slot = out_ref.at[core, a1, a2, back[d], :, span(c)]
-        return copy(slot, slot, c, 1 + n_z + d, (turn[d], r))
-
     def g2(c, part):
-        slot = out_ref.at[core, a1, part, :, :, span(c)]
+        slot = pool.at[c, core, a1, part]
         return copy(slot, slot, c, 1 + 2 * n_z, (z, p2))
 
     def g1(c, part):
-        slot = out_ref.at[core, part, :, :, :, span(c)]
+        slot = pool.at[c, core, part]
         return copy(slot, slot, c, 2 + 2 * n_z, (z, p1))
 
     def g0(c, part):
-        slot = out_ref.at[part, :, :, :, :, span(c)]
+        slot = pool.at[c, part]
         return copy(slot, slot, c, 3 + 2 * n_z, (z, sibling))
 
-    def stage0(c):
-        @pl.when(core == 0)
-        def _():
-            c0(c, txt_ref).start()
-
-        @pl.when(core == 1)
-        def _():
-            c0(c, img_ref).start()
+    tile = rows // 3
+
+    def product(left, right, m, store):
+        columns = pl.ds(m * wide, wide)
+
+        def body(i, carry):
+            at = pl.ds(pl.multiple_of(i * tile, tile), tile)
+            store(
+                at,
+                jnp.dot(left[0][at, :], right[0][:, columns], preferred_element_type=jnp.float32)
+                + jnp.dot(left[1][at, :], right[1][:, columns], preferred_element_type=jnp.float32),
+            )
+            return carry
+
+        lax.fori_loop(0, rows // tile, body, 0)
+
+    def of_head(head, m, store):
+        if head == 0:
+            product((xi0, xi1), (di0, di1), m, store)
+        else:
+            product((xt0, xt1), (dt0, dt1), m, store)
+
+    def theirs(m):
+        def store(at, value):
+            give[m, at, :] = value
+
+        for mine in range(2):
+            @pl.when(core == mine)
+            def _():
+                of_head(1 - mine, m, store)
+
+        c0(m).start()
+
+    def ours(m):
+        def store(at, value):
+            for j in range(per):
+                acc[m * per + j, at, :] = value[:, j * width : (j + 1) * width]
+
+        for mine in range(2):
+            @pl.when(core == mine)
+            def _():
+                of_head(mine, m, store)
 
     def stage1(c):
-        c0(c, img_ref).wait()
-
-        def add(ref):
-            s1[:, span(c)] = (ref[give1, span(c)] + got0[give1, span(c)]).astype(s1.dtype)
-            c1(c).start()
-            acc[keep1, span(c)] = ref[keep1, span(c)] + got0[keep1, span(c)]
-
-        @pl.when(core == 0)
-        def _():
-            add(img_ref)
-
-        @pl.when(core == 1)
-        def _():
-            add(txt_ref)
+        m, part = c // per, pl.ds(c % per * width, width)
+        if c % per == 0:
+            c0(m).wait()
+        s1[c] = (acc[c, give1, :] + got0[m, give1, part]).astype(s1.dtype)
+        c1(c).start()
+        acc[c, keep1, :] = acc[c, keep1, :] + got0[m, keep1, part]
 
     def stage2(c):
         c1(c).wait()
-        other2 = of((1 - a2) * quarter, quarter, 16)
-        s2[:, span(c)] = (acc[give2, span(c)] + r1[other2, span(c)].astype(jnp.float32)).astype(s2.dtype)
+        acc[c, give2, :] = acc[c, give2, :] + r1[c, other2, :].astype(jnp.float32)
         c2(c).start()
-        own2 = of(a2 * quarter, quarter, 16)
-        acc[keep2, span(c)] = acc[keep2, span(c)] + r1[own2, span(c)].astype(jnp.float32)
+        acc[c, keep2, :] = acc[c, keep2, :] + r1[c, own2, :].astype(jnp.float32)
 
     def stage3(c):
         c2(c).wait()
-        acc[keep2, span(c)] = acc[keep2, span(c)] + r2[:, span(c)].astype(jnp.float32)
+        acc[c, keep2, :] = acc[c, keep2, :] + r2[c]
         for d in range(1, n_z):
             c3(c, d).start()
 
     def stage4(c):
-        total = acc[of(base2 + z * piece, piece, 8), span(c)]
+        total = acc[c, of(base2 + z * piece, piece, 8), :]
         for d in range(1, n_z):
             c3(c, d).wait()
-            total = total + r3[d, :, span(c)]
+            total = total + r3[c, d]
         if padded > piece:
             total = jnp.concatenate([total, jnp.zeros((padded - piece, width), jnp.float32)], axis=0)
-        out_ref[core, a1, a2, z, :, span(c)] = total.astype(out_ref.dtype)
-        for d in range(1, n_z):
-            g3(c, d).start()
+        pool[c, core, a1, a2, z] = total.astype(pool.dtype)
+        for d in range(1, n_z):
+            g3(c, d, z).start()
 
     def stage5(c):
         for d in range(1, n_z):
-            g3_in(c, d).wait_recv()
+            g3(c, d, back[d]).wait_recv()
         g2(c, a2).start()
 
     def stage6(c):
@@ -228,50 +249,57 @@
 
     def stage8(c):
         g0(c, 1 - core).wait_recv()
-        for d in range(1, n_z):
-            g3(c, d).wait_send()
+        for head, ref in ((0, img_ref), (1, txt_ref)):
+            for k in range(4 * n_z):
+                value = pool[c, head, k // (2 * n_z), k // n_z % 2, k % n_z].astype(jnp.float32)
+                ref[k * piece : (k + 1) * piece, c * width : (c + 1) * width] = value[:piece]
+        for d in range(1, n_z):
+            g3(c, d, z).wait_send()
         g2(c, a2).wait_send()
         g1(c, a1).wait_send()
         g0(c, core).wait_send()
 
-    for c in range(CHUNKS):
-        stage0(c)
+    for m in range(panels):
+        theirs(m)
     stages = [stage1, stage2, stage3, stage4, stage5, stage6, stage7, stage8]
-    for tick in range(CHUNKS + len(stages) - 1):
+    for tick in range(chunks + len(stages) - 1):
+        if tick < chunks and tick % per == 0:
+            ours(tick // per)
         for at in range(len(stages)):
-            if 0 <= tick - at < CHUNKS:
+            if 0 <= tick - at < chunks:
                 stages[at](tick - at)
 
 
-def reduce_all(grad_img, grad_txt, n_z):
-    rows, cols = grad_img.shape
+def reduce_all(operands, n_z):
+    rows, cols = operands[0].shape[0], operands[4].shape[1]
     half, quarter = rows // 2, rows // 4
     piece = quarter // n_z
     padded = -(-piece // PAD) * PAD
-    low = jnp.bfloat16
-    out = pl.pallas_call(
+    chunks, width = cols // WIDTH, WIDTH
+    panels = chunks // 3
+    low, full = jnp.bfloat16, jnp.float32
+    return pl.pallas_call(
         functools.partial(reduce_kernel, n_z),
-        out_shape=jax.ShapeDtypeStruct((2, 2, 2, n_z, padded, cols), low),
-        in_specs=[pl.BlockSpec(memory_space=pltpu.VMEM)] * 2,
-        out_specs=pl.BlockSpec(memory_space=pltpu.VMEM),
+        out_shape=[jax.ShapeDtypeStruct((rows, cols), full)] * 2,
+        in_specs=[pl.BlockSpec(memory_space=pltpu.VMEM)] * 8,
+        out_specs=[pl.BlockSpec(memory_space=pltpu.VMEM)] * 2,
         scratch_shapes=[
-            pltpu.VMEM((rows, cols), jnp.float32),
-            pltpu.VMEM((rows, cols), jnp.float32),
-            pltpu.VMEM((half, cols), low),
-            pltpu.VMEM((half, cols), low),
-            pltpu.VMEM((quarter, cols), low),
-            pltpu.VMEM((quarter, cols), low),
-            pltpu.VMEM((n_z, piece, cols), jnp.float32),
-            pltpu.SemaphoreType.DMA((CHUNKS, 4 + 2 * n_z)),
-            pltpu.SemaphoreType.DMA((CHUNKS, 4 + 2 * n_z)),
+            pltpu.VMEM((panels, rows, 3 * width), full),
+            pltpu.VMEM((panels, rows, 3 * width), full),
+            pltpu.VMEM((chunks, rows, width), full),
+            pltpu.VMEM((chunks, half, width), low),
+            pltpu.VMEM((chunks, half, width), low),
+            pltpu.VMEM((chunks, quarter, width), full),
+            pltpu.VMEM((chunks, n_z, piece, width), full),
+            pltpu.VMEM((chunks, 2, 2, 2, n_z, padded, width), low),
+            pltpu.SemaphoreType.DMA((chunks, 4 + 2 * n_z)),
+            pltpu.SemaphoreType.DMA((chunks, 4 + 2 * n_z)),
         ],
         compiler_params=pltpu.CompilerParams(
-            collective_id=0, has_side_effects=True, vmem_limit_bytes=50 * 1024 * 1024
+            collective_id=0, has_side_effects=True, vmem_limit_bytes=58 * 1024 * 1024
         ),
-        cost_estimate=pl.CostEstimate(flops=10**9, bytes_accessed=10**8, transcendentals=0),
-    )(grad_img, grad_txt)
-    by_core = [out[c, :, :, :, :piece].astype(jnp.float32) for c in range(2)]
-    return tuple(part.reshape(rows, cols) for part in by_core)
+        cost_estimate=pl.CostEstimate(flops=6 * 10**9, bytes_accessed=10**8, transcendentals=0),
+    )(*operands)
 
 
 def tile_local(
@@ -305,19 +333,14 @@
 
     pieces = [[resid(a, b) for b in range(2)] for a in range(2)]
 
-    def grad_of(rows, own, upstream):
-        return sum(
-            across_rows(rows[k], unnormalize(own[k][0], own[k][2], upstream[k])) for k in range(2)
-        )
-
     d_img = [
         sum(jnp.dot(pieces[a][b], texts[b][1], preferred_element_type=jnp.float32) for b in range(2))
         for a in range(2)
     ]
     d_txt = [sum(across_rows(pieces[a][b], images[a][1]) for a in range(2)) for b in range(2)]
-    grad_img = grad_of(photos, images, d_img)
-    grad_txt = grad_of(wordings, texts, d_txt)
-    return reduce_all(grad_img, grad_txt, 4)
+    lefts = [rows.T for rows in photos + wordings]
+    rights = [unnormalize(own[0], own[2], up) for own, up in zip(images + texts, d_img + d_txt)]
+    return tuple(reduce_all(lefts + rights, 4))
 
 
 def solution(mesh):

time: 194 us -> 180 us (0.928)
  matrix products: 43 us -> 27.4 us
  local copies, waits for them, and re-layouts: 4.19 us -> 14.5 us
  waiting for transfers between devices: 38.4 us -> 34.1 us
  Pallas kernels: 93 us -> 90.5 us
    dot_general x8 -> x4, matrix products: 19.6 us -> 4.07 us  [across_rows(): lax.dot_general(left, right, (((0,), (0,)), ((), ())), preferred_element_...]
    unnamed x14 -> x16, local copies, waits for them, and re-layouts: 1.22 us -> 14.5 us
    ppermute x1, waiting for transfers between devices: 38.4 us -> 33.7 us  [tile_local(): photos = [photo_features[0], lax.ppermute(photo_features[0], 'blk', swap1)]]
    slice x1 -> x0, local copies, waits for them, and re-layouts: 2.97 us -> none  [reduce_all(): by_core = [out[c, :, :, :, :piece].astype(jnp.float32) for c in range(2)]]
    pallas_call x1, Pallas kernels: 93 us -> 90.5 us  [reduce_all(): pl.pallas_call(functools.partial(reduce_kernel, n_z), out_shape=[jax.Shap...]
    convert_element_type x2 -> x4, other arithmetic: 5.85 us -> 5.82 us  [unnormalize(): return (inverse * (upstream - unit * inner)).astype(jnp.bfloat16)]
  transfers between devices with their start and end apart: 3 -> 3, of which waited for: 1 -> 2; matrix products, arithmetic and copies ran while one was open for 11% -> 13% of each run, Pallas kernels for 0% -> 0%
where the time goes in v2:
time: 180 us
  Pallas kernels  90.5 us (50%)
  waiting for transfers between devices  34.1 us (19%)
  matrix products  27.4 us (15%)
  local copies, waits for them, and re-layouts  14.5 us (8%)
  other arithmetic  6.6 us (4%)
  starting transfers between devices  4.6 us (3%)
  between operations  2.1 us (1%)
    pallas_call x1, Pallas kernels, reduce_all(): pl.pallas_call(functools.partial(reduce_kernel, n_z), out_shape=[jax.Shap...  90.5 us
    ppermute x1, waiting for transfers between devices, tile_local(): photos = [photo_features[0], lax.ppermute(photo_features[0], 'blk', swap1)]  33.7 us
    dot_general x4, matrix products, normalize(): projected = jnp.dot(features, head, preferred_element_type=jnp.float32)  15.1 us
    unnamed x16, local copies, waits for them, and re-layouts  14.5 us
    convert_element_type x4, other arithmetic, unnormalize(): return (inverse * (upstream - unit * inner)).astype(jnp.bfloat16)  5.82 us
    dot_general x4, matrix products, resid(): lax.dot_general(images[a][1], texts[b][1], (((1,), (1,)), ((), ())), pref...  4.37 us
    dot_general x4, matrix products, across_rows(): lax.dot_general(left, right, (((0,), (0,)), ((), ())), preferred_element_...  4.07 us
    dot_general x4, matrix products, tile_local(): jnp.dot(pieces[a][b], texts[b][1], preferred_element_type=jnp.float32)  3.91 us
  transfers between devices with their start and end apart: 3, of which 2 were waited for; matrix products, arithmetic and copies ran while one was open for 13% of the time, Pallas kernels for 0%

profile of v2, /device:TPU:1, one launch (start us, length us, event | category | flops | bytes accessed | tf_op | source)
XLA Modules:
  0.0 179.8 jit_solution(11590484105622217446)
XLA Ops:
  0.7 2.5 %copy.9 = bf16[1,512,1152]{1,2,0:T(8,128)(2,1)} copy(bf16[1,512,1152]{2,1,0:T(8,128)(2,1)} %param.7) | data formatting | bytes 2359296 | tf_op args[0]
  3.2 2.1 %collective-permute-start = (bf16[512,1152]{0,1:T(8,128)(2,1)}, bf16[512,1152]{0,1:T(8,128)(2,1)}, u32[]{:S(2)}, u32[]{:S(2)}) collective-permute-start(bf16[512,1152]{0,1:T(8,128)(2,1)} %bitcast.60), channel_id=1, source_target_pairs={{0,8},{8,0},{16,24},{24,16},{1,9},{9,1},{17,25},{25,17},{2,10},{10... | collective-permute-start | bytes 3538952 | tf_op jit(solution)/shard_map/ppermute | solution.py:318
  5.3 2.4 %copy.10 = bf16[1,512,1152]{1,2,0:T(8,128)(2,1)} copy(bf16[1,512,1152]{2,1,0:T(8,128)(2,1)} %param.8) | data formatting | bytes 2359296 | tf_op args[1]
  7.7 2.3 %collective-permute-start.1 = (bf16[512,1152]{0,1:T(8,128)(2,1)}, bf16[512,1152]{0,1:T(8,128)(2,1)}, u32[]{:S(2)}, u32[]{:S(2)}) collective-permute-start(bf16[512,1152]{0,1:T(8,128)(2,1)} %bitcast.62), channel_id=1, source_target_pairs={{0,16},{8,24},{16,0},{24,8},{1,17},{9,25},{17,1},{25,9},{2,18},{10... | collective-permute-start | bytes 3538952 | tf_op jit(solution)/shard_map/ppermute | solution.py:319
  10.2 5.4 %multiply_reduce_fusion.6 = (f32[512]{0:T(512)S(1)}, f32[512,1152]{1,0:T(8,128)}) fusion(bf16[1152,1152]{1,0:T(8,128)(2,1)} %param.11, bf16[1,512,1152]{2,1,0:T(8,128)(2,1)} %param.8), kind=kOutput, calls=%fused_computation.14 | convolution fusion | flops 1360133632 | bytes 6195200 | tf_op jit(solution)/shard_map/dot_general | solution.py:26
  16.9 3.2 %multiply_reduce_fusion.7 = (f32[512]{0:T(512)S(1)}, f32[512,1152]{1,0:T(8,128)S(1)}) fusion(bf16[1152,1152]{1,0:T(8,128)(2,1)S(1)} %copy-done, bf16[1,512,1152]{2,1,0:T(8,128)(2,1)} %param.7), kind=kOutput, calls=%fused_computation.15 | convolution fusion | flops 1360133632 | bytes 6195200 | tf_op jit(solution)/shard_map/dot_general | solution.py:26
  20.4 33.7 %collective-permute-done = bf16[512,1152]{0,1:T(8,128)(2,1)} collective-permute-done((bf16[512,1152]{0,1:T(8,128)(2,1)}, bf16[512,1152]{0,1:T(8,128)(2,1)}, u32[]{:S(2)}, u32[]{:S(2)}) %collective-permute-start) | collective-permute-done | bytes 1179680 | tf_op jit(solution)/shard_map/ppermute | solution.py:318
  54.0 3.2 %multiply_reduce_fusion.3 = (f32[512]{0:T(512)S(1)}, f32[512,1152]{1,0:T(8,128)S(1)}) fusion(bf16[512,1152]{0,1:T(8,128)(2,1)} %collective-permute-done, bf16[1152,1152]{1,0:T(8,128)(2,1)S(1)} %copy-done), kind=kOutput, calls=%fused_computation.10 | convolution fusion | flops 1360133632 | bytes 6195200 | tf_op jit(solution)/shard_map/dot_general | solution.py:26
  57.3 0.3 multiply_convert_fusion.4
  57.6 1.1 fusion.25
  58.7 0.9 fusion.32
  59.6 0.8 fusion.30
  60.5 0.4 collective-permute-done.1
  60.9 0.5 copy-done.4
  61.4 3.3 %multiply_reduce_fusion.5 = (f32[512]{0:T(512)S(1)}, f32[512,1152]{1,0:T(8,128)S(1)}) fusion(bf16[512,1152]{0,1:T(8,128)(2,1)} %collective-permute-done.1, bf16[1152,1152]{1,0:T(8,128)(2,1)S(1)} %copy-done.4), kind=kOutput, calls=%fused_computation.13 | convolution fusion | flops 1360133632 | bytes 6195200 | tf_op jit(solution)/shard_map/dot_general | solution.py:26
  64.9 1.1 fusion.24
  66.0 0.9 fusion.33
  66.8 1.1 multiply_convert_fusion.9
  67.9 1.0 fusion.31
  69.0 1.2 multiply_reduce_fusion.1
  70.2 1.1 multiply_convert_fusion.8
  71.3 1.1 multiply_reduce_fusion
  72.4 1.0 multiply_reduce_fusion.2
  73.4 1.0 multiply_reduce_fusion.4
  74.4 1.5 multiply_convert_fusion.dt1
  75.9 1.5 multiply_convert_fusion.1.dt0
  77.4 1.5 multiply_convert_fusion.2.di1
  78.8 1.4 multiply_convert_fusion.3.di0
  80.3 90.5 %shard_map.86 = (f32[1152,1152]{1,0:T(8,128)}, f32[1152,1152]{1,0:T(8,128)}) custom-call(bf16[1152,512]{1,0:T(8,128)(2,1)} %bitcast.61, bf16[1152,512]{1,0:T(8,128)(2,1)} %bitcast.2.xi1, bf16[1152,512]{1,0:T(8,128)(2,1)} %bitcast.63, bf16[1152,512]{1,0:T(8,128)(2,1)} %bitcast.5.xt1, bf16[512,1152]{1,0:T(8,128)(2,1)} %multiply_convert_fusion.3.di0, ...), custom_call_target="tpu_custom_call" | custom-call | flops 6000000000 | bytes 100000000 | tf_op jit(solution)/shard_map/pallas_call | solution.py:281
  170.8 5.4 %copy.15 = f32[1152,1152]{1,0:T(8,128)} copy(f32[1152,1152]{1,0:T(8,128)} %get-tuple-element.22) | data formatting | bytes 10616832
  176.2 2.7 %copy.16 = f32[1152,1152]{1,0:T(8,128)} copy(f32[1152,1152]{1,0:T(8,128)S(1)} %copy-done.3) | data formatting | bytes 10616832
  178.9 1.0 copy-done.1
  (20 shorter events, 0.7 us)
Async XLA Ops:
  0.6 16.3 %copy-start = (bf16[1152,1152]{1,0:T(8,128)(2,1)S(1)}, bf16[1152,1152]{1,0:T(8,128)(2,1)}, u32[]{:S(2)}) copy-start(bf16[1152,1152]{1,0:T(8,128)(2,1)} %param.10) | copy-start | bytes 7962628
  0.6 9.4 %copy-start.5 = (s32[1,512]{1,0:T(1,128)S(1)}, s32[1,512]{1,0:T(1,128)}, u32[]{:S(2)}) copy-start(s32[1,512]{1,0:T(1,128)} %param.9) | copy-start | bytes 6148
  3.2 50.9 %collective-permute-start = (bf16[512,1152]{0,1:T(8,128)(2,1)}, bf16[512,1152]{0,1:T(8,128)(2,1)}, u32[]{:S(2)}, u32[]{:S(2)}) collective-permute-start(bf16[512,1152]{0,1:T(8,128)(2,1)} %bitcast.60), channel_id=1, source_target_pairs={{0,8},{8,0},{16,24},{24,16},{1,9},{9,1},{17,25},{25,17},{2,10},{10... | collective-permute-start | bytes 3538952 | tf_op jit(solution)/shard_map/ppermute | solution.py:318
  7.7 53.1 %collective-permute-start.1 = (bf16[512,1152]{0,1:T(8,128)(2,1)}, bf16[512,1152]{0,1:T(8,128)(2,1)}, u32[]{:S(2)}, u32[]{:S(2)}) collective-permute-start(bf16[512,1152]{0,1:T(8,128)(2,1)} %bitcast.62), channel_id=1, source_target_pairs={{0,16},{8,24},{16,0},{24,8},{1,17},{9,25},{17,1},{25,9},{2,18},{10... | collective-permute-start | bytes 3538952 | tf_op jit(solution)/shard_map/ppermute | solution.py:319
  10.1 56.8 %collective-permute-start.2 = (s32[512]{0:T(512)S(1)}, s32[512]{0:T(512)S(1)}, u32[]{:S(2)}, u32[]{:S(2)}) collective-permute-start(s32[512]{0:T(512)S(1)} %bitcast.64), channel_id=1, source_target_pairs={{0,8},{8,0},{16,24},{24,16},{1,9},{9,1},{17,25},{25,17},{2,10},{10... | collective-permute-start | bytes 6152 | tf_op jit(solution)/shard_map/ppermute | solution.py:320
  20.4 36.9 %copy-start.2 = (f32[512,1152]{1,0:T(8,128)S(1)}, f32[512,1152]{1,0:T(8,128)}, u32[]{:S(2)}) copy-start(f32[512,1152]{1,0:T(8,128)} %get-tuple-element.5) | copy-start | bytes 7077892
  59.6 1.8 copy-start.4
  170.8 5.4 %copy-start.3 = (f32[1152,1152]{1,0:T(8,128)S(1)}, f32[1152,1152]{1,0:T(8,128)}, u32[]{:S(2)}) copy-start(f32[1152,1152]{1,0:T(8,128)} %get-tuple-element.23) | copy-start | bytes 15925252
  176.2 3.7 %copy-start.1 = (bf16[1152,1152]{1,0:T(8,128)(2,1)S(1)}, bf16[1152,1152]{1,0:T(8,128)(2,1)}, u32[]{:S(2)}) copy-start(bf16[1152,1152]{1,0:T(8,128)(2,1)} %param.10) | copy-start | bytes 7962628

commit v3 on v2

--- a/solution.py
+++ b/solution.py
@@ -169,8 +169,8 @@
             at = pl.ds(pl.multiple_of(i * tile, tile), tile)
             store(
                 at,
-                jnp.dot(left[0][at, :], right[0][:, columns], preferred_element_type=jnp.float32)
-                + jnp.dot(left[1][at, :], right[1][:, columns], preferred_element_type=jnp.float32),
+                across_rows(left[0][:, at], right[0][:, columns])
+                + across_rows(left[1][:, at], right[1][:, columns]),
             )
             return carry
 
@@ -271,7 +271,7 @@
 
 
 def reduce_all(operands, n_z):
-    rows, cols = operands[0].shape[0], operands[4].shape[1]
+    rows, cols = operands[0].shape[1], operands[4].shape[1]
     half, quarter = rows // 2, rows // 4
     piece = quarter // n_z
     padded = -(-piece // PAD) * PAD
@@ -338,7 +338,7 @@
         for a in range(2)
     ]
     d_txt = [sum(across_rows(pieces[a][b], images[a][1]) for a in range(2)) for b in range(2)]
-    lefts = [rows.T for rows in photos + wordings]
+    lefts = photos + wordings
     rights = [unnormalize(own[0], own[2], up) for own, up in zip(images + texts, d_img + d_txt)]
     return tuple(reduce_all(lefts + rights, 4))
 

time: 180 us -> 182 us (1.011)
  waiting for transfers between devices: 34.1 us -> 38.5 us
  local copies, waits for them, and re-layouts: 14.5 us -> 10.3 us
    ppermute x1, waiting for transfers between devices: 33.7 us -> 38.5 us  [tile_local(): photos = [photo_features[0], lax.ppermute(photo_features[0], 'blk', swap1)]]
    unnamed x16 -> x14, local copies, waits for them, and re-layouts: 14.5 us -> 10.3 us
  transfers between devices with their start and end apart: 3 -> 3, of which waited for: 2 -> 1; matrix products, arithmetic and copies ran while one was open for 13% -> 11% of each run, Pallas kernels for 0% -> 0%
where the time goes in v3:
time: 182 us
  Pallas kernels  91.9 us (50%)
  waiting for transfers between devices  38.5 us (21%)
  matrix products  27.5 us (15%)
  local copies, waits for them, and re-layouts  10.3 us (6%)
  other arithmetic  6.57 us (4%)
  starting transfers between devices  4.67 us (3%)
  between operations  2.12 us (1%)
    pallas_call x1, Pallas kernels, reduce_all(): pl.pallas_call(functools.partial(reduce_kernel, n_z), out_shape=[jax.Shap...  91.9 us
    ppermute x1, waiting for transfers between devices, tile_local(): photos = [photo_features[0], lax.ppermute(photo_features[0], 'blk', swap1)]  38.5 us
    dot_general x4, matrix products, normalize(): projected = jnp.dot(features, head, preferred_element_type=jnp.float32)  15.1 us
    unnamed x14, local copies, waits for them, and re-layouts  10.3 us
    convert_element_type x4, other arithmetic, unnormalize(): return (inverse * (upstream - unit * inner)).astype(jnp.bfloat16)  5.8 us
    dot_general x4, matrix products, resid(): lax.dot_general(images[a][1], texts[b][1], (((1,), (1,)), ((), ())), pref...  4.37 us
    dot_general x4, matrix products, across_rows(): lax.dot_general(left, right, (((0,), (0,)), ((), ())), preferred_element_...  4.07 us
    dot_general x4, matrix products, tile_local(): jnp.dot(pieces[a][b], texts[b][1], preferred_element_type=jnp.float32)  3.91 us
  transfers between devices with their start and end apart: 3, of which 1 were waited for; matrix products, arithmetic and copies ran while one was open for 11% of the time, Pallas kernels for 0%

profile of v3, /device:TPU:1, one launch (start us, length us, event | category | flops | bytes accessed | tf_op | source)
XLA Modules:
  0.0 181.6 jit_solution(10542179304748690224)
XLA Ops:
  0.6 3.2 %collective-permute-start.1 = (bf16[512,1152]{1,0:T(8,128)(2,1)}, bf16[512,1152]{1,0:T(8,128)(2,1)}, u32[]{:S(2)}, u32[]{:S(2)}) collective-permute-start(bf16[512,1152]{1,0:T(8,128)(2,1)} %bitcast.54), channel_id=1, source_target_pairs={{0,16},{8,24},{16,0},{24,8},{1,17},{9,25},{17,1},{25,9},{2,18},{10... | collective-permute-start | bytes 3538952 | tf_op jit(solution)/shard_map/ppermute | solution.py:319
  3.9 1.3 collective-permute-start
  5.3 4.5 %multiply_reduce_fusion.7 = (f32[512]{0:T(512)S(1)}, f32[512,1152]{1,0:T(8,128)}) fusion(bf16[1152,1152]{1,0:T(8,128)(2,1)S(1)} %copy-done, bf16[1,512,1152]{2,1,0:T(8,128)(2,1)} %param.7), kind=kOutput, calls=%fused_computation.15 | convolution fusion | flops 1360133632 | bytes 6195200 | tf_op jit(solution)/shard_map/dot_general | solution.py:26
  11.2 4.2 %multiply_reduce_fusion.6 = (f32[512]{0:T(512)S(1)}, f32[512,1152]{1,0:T(8,128)S(1)}) fusion(bf16[1152,1152]{1,0:T(8,128)(2,1)} %param.11, bf16[1,512,1152]{2,1,0:T(8,128)(2,1)} %param.8), kind=kOutput, calls=%fused_computation.14 | convolution fusion | flops 1360133632 | bytes 6195200 | tf_op jit(solution)/shard_map/dot_general | solution.py:26
  15.4 0.2 multiply_convert_fusion.7
  15.6 38.5 %collective-permute-done.xi1 = bf16[512,1152]{1,0:T(8,128)(2,1)} collective-permute-done((bf16[512,1152]{1,0:T(8,128)(2,1)}, bf16[512,1152]{1,0:T(8,128)(2,1)}, u32[]{:S(2)}, u32[]{:S(2)}) %collective-permute-start) | collective-permute-done | bytes 1179680 | tf_op jit(solution)/shard_map/ppermute | solution.py:318
  54.1 3.2 %multiply_reduce_fusion.3 = (f32[512]{0:T(512)S(1)}, f32[512,1152]{1,0:T(8,128)S(1)}) fusion(bf16[512,1152]{1,0:T(8,128)(2,1)} %collective-permute-done.xi1, bf16[1152,1152]{1,0:T(8,128)(2,1)S(1)} %copy-done), kind=kOutput, calls=%fused_computation.10 | convolution fusion | flops 1360133632 | bytes 6195200 | tf_op jit(solution)/shard_map/dot_general | solution.py:26
  57.3 0.3 multiply_convert_fusion.4
  57.7 0.3 copy-done.5
  58.0 1.1 fusion.25
  59.1 0.9 fusion.32
  60.0 0.8 fusion.30
  60.9 0.9 copy-done.4
  61.7 3.2 %multiply_reduce_fusion.5 = (f32[512]{0:T(512)S(1)}, f32[512,1152]{1,0:T(8,128)S(1)}) fusion(bf16[512,1152]{1,0:T(8,128)(2,1)} %collective-permute-done.1.xt1, bf16[1152,1152]{1,0:T(8,128)(2,1)S(1)} %copy-done.4), kind=kOutput, calls=%fused_computation.13 | convolution fusion | flops 1360133632 | bytes 6195200 | tf_op jit(solution)/shard_map/dot_general | solution.py:26
  65.0 0.2 multiply_convert_fusion.5
  65.2 1.1 fusion.24
  66.3 0.9 fusion.33
  67.2 1.1 multiply_convert_fusion.9
  68.3 1.0 fusion.31
  69.3 1.2 multiply_reduce_fusion.1
  70.5 1.1 multiply_convert_fusion.8
  71.6 1.1 multiply_reduce_fusion
  72.8 1.0 multiply_reduce_fusion.2
  73.8 1.0 multiply_reduce_fusion.4
  74.8 1.5 multiply_convert_fusion.dt1
  76.2 1.5 multiply_convert_fusion.1.dt0
  77.7 1.4 multiply_convert_fusion.2.di1
  79.2 1.4 multiply_convert_fusion.3.di0
  80.6 91.9 %shard_map.86 = (f32[1152,1152]{1,0:T(8,128)}, f32[1152,1152]{1,0:T(8,128)}) custom-call(bf16[512,1152]{1,0:T(8,128)(2,1)} %bitcast.53, bf16[512,1152]{1,0:T(8,128)(2,1)} %collective-permute-done.xi1, bf16[512,1152]{1,0:T(8,128)(2,1)} %bitcast.55, bf16[512,1152]{1,0:T(8,128)(2,1)} %collective-permute-done.1.xt1, ...), custom_call_target="tpu_custom_call" | custom-call | flops 6000000000 | bytes 100000000 | tf_op jit(solution)/shard_map/pallas_call | solution.py:281
  172.6 5.4 %copy.13 = f32[1152,1152]{1,0:T(8,128)} copy(f32[1152,1152]{1,0:T(8,128)} %get-tuple-element.22) | data formatting | bytes 10616832
  177.9 2.7 %copy.14 = f32[1152,1152]{1,0:T(8,128)} copy(f32[1152,1152]{1,0:T(8,128)S(1)} %copy-done.3) | data formatting | bytes 10616832
  180.6 1.0 copy-done.1
  (18 shorter events, 0.2 us)
Async XLA Ops:
  0.6 4.7 %copy-start = (bf16[1152,1152]{1,0:T(8,128)(2,1)S(1)}, bf16[1152,1152]{1,0:T(8,128)(2,1)}, u32[]{:S(2)}) copy-start(bf16[1152,1152]{1,0:T(8,128)(2,1)} %param.10) | copy-start | bytes 7962628
  0.6 60.2 %collective-permute-start.1 = (bf16[512,1152]{1,0:T(8,128)(2,1)}, bf16[512,1152]{1,0:T(8,128)(2,1)}, u32[]{:S(2)}, u32[]{:S(2)}) collective-permute-start(bf16[512,1152]{1,0:T(8,128)(2,1)} %bitcast.54), channel_id=1, source_target_pairs={{0,16},{8,24},{16,0},{24,8},{1,17},{9,25},{17,1},{25,9},{2,18},{10... | collective-permute-start | bytes 3538952 | tf_op jit(solution)/shard_map/ppermute | solution.py:319
  3.9 50.3 %collective-permute-start = (bf16[512,1152]{1,0:T(8,128)(2,1)}, bf16[512,1152]{1,0:T(8,128)(2,1)}, u32[]{:S(2)}, u32[]{:S(2)}) collective-permute-start(bf16[512,1152]{1,0:T(8,128)(2,1)} %bitcast.52), channel_id=1, source_target_pairs={{0,8},{8,0},{16,24},{24,16},{1,9},{9,1},{17,25},{25,17},{2,10},{10... | collective-permute-start | bytes 3538952 | tf_op jit(solution)/shard_map/ppermute | solution.py:318
  5.1 62.0 %collective-permute-start.2 = (s32[512]{0:T(512)}, s32[512]{0:T(512)S(1)}, u32[]{:S(2)}, u32[]{:S(2)}) collective-permute-start(s32[512]{0:T(512)} %bitcast.56), channel_id=1, source_target_pairs={{0,8},{8,0},{16,24},{24,16},{1,9},{9,1},{17,25},{25,17},{2,10},{10... | collective-permute-start | bytes 6152 | tf_op jit(solution)/shard_map/ppermute | solution.py:320
  11.2 4.2 %copy-start.2 = (f32[512,1152]{1,0:T(8,128)S(1)}, f32[512,1152]{1,0:T(8,128)}, u32[]{:S(2)}) copy-start(f32[512,1152]{1,0:T(8,128)} %get-tuple-element.3) | copy-start | bytes 7077892
  57.3 0.7 copy-start.5
  60.0 1.8 copy-start.4
  172.5 5.4 %copy-start.3 = (f32[1152,1152]{1,0:T(8,128)S(1)}, f32[1152,1152]{1,0:T(8,128)}, u32[]{:S(2)}) copy-start(f32[1152,1152]{1,0:T(8,128)} %get-tuple-element.23) | copy-start | bytes 15925252
  177.9 3.7 %copy-start.1 = (bf16[1152,1152]{1,0:T(8,128)(2,1)S(1)}, bf16[1152,1152]{1,0:T(8,128)(2,1)}, u32[]{:S(2)}) copy-start(bf16[1152,1152]{1,0:T(8,128)(2,1)} %param.10) | copy-start | bytes 7962628
